TPU v7x, 768 devices: a whole 4x8x12 slice. The times are simulated.
768 devices in a mesh: row: 24 (over y, z_lo), col: 32 (over x, z_hi, core).
Axes of the slice: x: 4, y: 8, z: 12 (z_hi: 4, z_lo: 3; z = z_hi * 3 + z_lo), core: 2. Of those that a mesh axis runs over, the one named last changes fastest.
Arguments:
- features: bfloat16 [98304, 512], P(('col', 'row')), may hold values from -6 to 6
- tile_values: bfloat16 [12288, 256, 256], P(('row', 'col')), as said below
- tile_rows: int32 [12288], P(('row', 'col')), may hold values from 0 to 15
- tile_cols: int32 [12288], P(('row', 'col')), may hold values from 0 to 11
- tile_live: int32 [768], P(('row', 'col')), may hold values from 4 to 16, as said below
- weight: bfloat16 [512, 512], replicated, may hold values from -0.25 to 0.25
- cotangent: bfloat16 [98304, 512], P(('row', 'col')), may hold values from -6 to 6
Outputs:
- hidden: bfloat16 [98304, 512], P(('row', 'col'))
- grad_features: bfloat16 [98304, 512], P(('col', 'row'))
- grad_weight: float32 [512, 512], replicated
Inputs may be any that keep to these rules, and one draw needn't show every extreme that they name: `tile_live`: each block has 4 to 16 nonempty slots; some block has exactly 16 in every draw. `tile_values`: edge weights are non-negative.
All inputs are finite; a program needn't handle non-finite values.
Results may differ from a plain program's by a relative error of at most 0.02.
Values may be sent and summed in bfloat16 or wider, within the bound.
A program may use at most 128 MiB of HBM per device.

v0:
```python
import jax
import jax.numpy as jnp
from jax import lax
from jax.sharding import PartitionSpec as P


def shards(features, tile_values, tile_rows, tile_cols, tile_live, weight, cotangent):
    block_rows, feature_width = features.shape
    tile_edge = tile_values.shape[1]
    rows_count = lax.axis_size("row")
    cols_count = lax.axis_size("col")
    row_tiles = block_rows * cols_count // tile_edge
    col_tiles = block_rows * rows_count // tile_edge
    live_count = tile_live[0]
    column_block = lax.all_gather(features, "row", axis=0, tiled=True).reshape(
        col_tiles, tile_edge, feature_width
    )

    def forward_slot(slot_index, accumulated):
        tile_block = lax.dynamic_index_in_dim(tile_values, slot_index, 0, keepdims=False)
        source = lax.dynamic_index_in_dim(column_block, tile_cols[slot_index], 0, keepdims=False)
        product = jnp.dot(tile_block, source, preferred_element_type=jnp.float32)
        target = tile_rows[slot_index]
        current = lax.dynamic_index_in_dim(accumulated, target, 0, keepdims=False)
        return lax.dynamic_update_index_in_dim(accumulated, current + product, target, 0)

    summed = lax.fori_loop(
        0, live_count, forward_slot, jnp.zeros((row_tiles, tile_edge, feature_width), jnp.float32)
    )
    own_sum = lax.psum_scatter(
        summed.reshape(row_tiles * tile_edge, feature_width).astype(jnp.bfloat16),
        "col",
        scatter_dimension=0,
        tiled=True,
    )
    pre_act = jnp.dot(own_sum, weight, preferred_element_type=jnp.float32)
    sigmoid_z = jax.nn.sigmoid(pre_act)
    hidden = (pre_act * sigmoid_z).astype(jnp.bfloat16)
    own_grad = (
        cotangent.astype(jnp.float32) * sigmoid_z * (1.0 + pre_act * (1.0 - sigmoid_z))
    ).astype(jnp.bfloat16)
    grad_block = lax.all_gather(own_grad, "col", axis=0, tiled=True)
    local_term = jnp.einsum("nd,ne->de", own_sum, own_grad, preferred_element_type=jnp.float32)
    grad_weight = lax.psum(local_term, ("row", "col")) * float(
        block_rows * rows_count * cols_count
    ) ** (-0.5)
    grad_tiles = grad_block.reshape(row_tiles, tile_edge, feature_width)

    def backward_slot(slot_index, accumulated):
        tile_block = lax.dynamic_index_in_dim(tile_values, slot_index, 0, keepdims=False)
        source = lax.dynamic_index_in_dim(grad_tiles, tile_rows[slot_index], 0, keepdims=False)
        product = jnp.einsum("ji,jf->if", tile_block, source, preferred_element_type=jnp.float32)
        target = tile_cols[slot_index]
        current = lax.dynamic_index_in_dim(accumulated, target, 0, keepdims=False)
        return lax.dynamic_update_index_in_dim(accumulated, current + product, target, 0)

    backward_partial = lax.fori_loop(
        0, live_count, backward_slot, jnp.zeros((col_tiles, tile_edge, feature_width), jnp.float32)
    )
    backward_partial = backward_partial.reshape(col_tiles * tile_edge, feature_width)
    gathered_back = lax.psum_scatter(
        backward_partial.astype(jnp.bfloat16), "row", scatter_dimension=0, tiled=True
    )
    grad_features = jnp.einsum(
        "nd,ed->ne", gathered_back, weight, preferred_element_type=jnp.float32
    ).astype(jnp.bfloat16)
    return (hidden, grad_features, grad_weight)


def solution(mesh):
    return jax.shard_map(
        shards,
        mesh=mesh,
        in_specs=(
            P(("col", "row"), None),
            P(("row", "col"), None, None),
            P(("row", "col")),
            P(("row", "col")),
            P(("row", "col")),
            P(),
            P(("row", "col"), None),
        ),
        out_specs=(P(("row", "col"), None), P(("col", "row"), None), P()),
        check_vma=False,
    )
```

profile of v0, /device:TPU:198, one launch (start us, length us, event | category | flops | bytes accessed | tf_op | source)
XLA Modules:
  0.0 1137.3 jit_solution(566081048417943520)
XLA Ops:
  8.0 144.2 %all-gather.3.cloned.1.call-done = bf16[3072,512]{1,0:T(8,128)(2,1)} async-done(((bf16[128,512]{1,0:T(8,128)(2,1)}), bf16[3072,512]{1,0:T(8,128)(2,1)}) %all-gather.3.cloned.1.call-update) | async-done | bytes 3145744 | tf_op jit(solution)/shard_map/all_gather | solution.py:15
  152.2 4.3 broadcast_in_dim.14
  156.5 107.1 %while.20 = (s32[]{:T(128)}, f32[16,256,512]{2,1,0:T(8,128)}, s32[]{:T(128)}, s32[16]{0:T(128)S(1)}, bf16[16,256,256]{2,1,0:T(8,128)(2,1)}, /*index=5*/s32[16]{0...) while((s32[]{:T(128)}, f32[16,256,512]{2,1,0:T(8,128)}, ...), condition=%wide.region_1.2_spmd, body=%wide.region_0.1_spmd.sunk | while | flops 67239944 | bytes 2490619 | solution.py:27
  198.8 2.1 fusion.29
  263.6 6.0 convert_element_type.24
  269.6 156.7 %reduce-scatter.3.cloned.1.call-done = bf16[128,512]{1,0:T(8,128)(2,1)} async-done(((bf16[4096,512]{1,0:T(8,128)(2,1)}), bf16[128,512]{1,0:T(8,128)(2,1)}) %reduce-scatter.3.cloned.1.call-update) | async-done | bytes 131088 | tf_op jit(solution)/shard_map/reduce_scatter | solution.py:30
  428.4 2.3 fusion.14
  430.7 80.7 %all-gather.5.cloned.1.call-done = bf16[4096,512]{1,0:T(8,128)(2,1)} async-done(((bf16[128,512]{1,0:T(8,128)(2,1)}), bf16[4096,512]{1,0:T(8,128)(2,1)}) %all-gather.5.cloned.1.call-update) | async-done | bytes 4194320 | tf_op jit(solution)/shard_map/all_gather | solution.py:42
  511.4 3.4 broadcast_in_dim.15
  514.9 107.5 %while.21 = (s32[]{:T(128)}, f32[12,256,512]{2,1,0:T(8,128)}, s32[]{:T(128)}, s32[16]{0:T(128)S(1)}, bf16[16,256,256]{2,1,0:T(8,128)(2,1)}, /*index=5*/s32[16]{0...) while((s32[]{:T(128)}, f32[12,256,512]{2,1,0:T(8,128)}, ...), condition=%wide.region_4.5_spmd, body=%wide.region_3.4_spmd.sunk | while | flops 67239944 | bytes 2490619 | solution.py:57
  521.7 2.1 fusion.32
  539.5 2.1 fusion.32
  548.4 2.1 fusion.32
  557.3 2.1 fusion.32
  575.0 2.1 fusion.32
  584.0 2.1 fusion.32
  592.9 2.1 fusion.32
  601.8 2.1 fusion.32
  610.8 2.1 fusion.32
  619.7 2.1 fusion.32
  622.4 4.9 convert_element_type.29
  627.4 355.9 %all-reduce.2.cloned.1.call-done = f32[512,512]{1,0:T(8,128)} async-done(((f32[512,512]{1,0:T(8,128)}), f32[512,512]{1,0:T(8,128)}) %all-reduce.2.cloned.1.call-update) | async-done | bytes 1048592 | tf_op jit(solution)/shard_map/psum | solution.py:44
  983.3 2.3 broadcast_multiply_fusion
  985.6 143.3 %reduce-scatter.5.cloned.1.call-done = bf16[128,512]{1,0:T(8,128)(2,1)} async-done(((bf16[3072,512]{1,0:T(8,128)(2,1)}), bf16[128,512]{1,0:T(8,128)(2,1)}) %reduce-scatter.5.cloned.1.call-update) | async-done | bytes 131088 | tf_op jit(solution)/shard_map/reduce_scatter | solution.py:61
  (105 shorter events, 85.7 us)
Async XLA Ops:
  7.2 419.2 %copy-start = (bf16[512,512]{1,0:T(8,128)(2,1)S(1)}, bf16[512,512]{1,0:T(8,128)(2,1)}, u32[]{:S(2)}) copy-start(bf16[512,512]{1,0:T(8,128)(2,1)} %param.16) | copy-start | bytes 1572868
  7.2 149.3 %copy-start.2 = (s32[16]{0:T(128)S(1)}, s32[16]{0:T(128)}, u32[]{:S(2)}) copy-start(s32[16]{0:T(128)} %param.13) | copy-start | bytes 196
  7.2 149.3 %copy-start.3 = (s32[16]{0:T(128)S(1)}, s32[16]{0:T(128)}, u32[]{:S(2)}) copy-start(s32[16]{0:T(128)} %param.14) | copy-start | bytes 196
  7.2 145.0 %all-gather.3.cloned.1.call-start = ((), (), s32[]{:S(2)}) async-start(), calls=%async_computation.2 | async-start | bytes 3276800 | tf_op jit(solution)/shard_map/all_gather | solution.py:15
  7.9 418.4 %reduce-scatter.3.cloned.1.call-start = ((), (), s32[]{:S(2)}) async-start(), calls=%async_computation.3 | async-start | bytes 4325376 | tf_op jit(solution)/shard_map/reduce_scatter | solution.py:30
  263.6 162.8 %copy-start.1 = (bf16[128,512]{1,0:T(8,128)(2,1)S(1)}, bf16[128,512]{1,0:T(8,128)(2,1)}, u32[]{:S(2)}) copy-start(bf16[128,512]{1,0:T(8,128)(2,1)} %param.17) | copy-start | bytes 393220
  269.6 241.8 %all-gather.5.cloned.1.call-start = ((), (), s32[]{:S(2)}) async-start(), calls=%async_computation.4 | async-start | bytes 4325376 | tf_op jit(solution)/shard_map/all_gather | solution.py:42
  428.3 555.0 %all-reduce.2.cloned.1.call-start = ((), (), s32[]{:S(2)}) async-start(), calls=%async_computation.6 | async-start | bytes 2097152 | tf_op jit(solution)/shard_map/psum | solution.py:44
  430.6 698.2 %reduce-scatter.5.cloned.1.call-start = ((), (), s32[]{:S(2)}) async-start(), calls=%async_computation.5 | async-start | bytes 3276800 | tf_op jit(solution)/shard_map/reduce_scatter | solution.py:61
Sparse Core Ops, SparseCore 0:
  10.4 141.6 all-gather.2
  269.7 156.5 reduce-scatter.2
  431.3 80.1 all-gather.4
  518.1 465.1 all-reduce.1
  986.3 142.5 reduce-scatter.4
where the time goes:
time: 1140 us
  waiting for transfers between devices  882 us (77%)
  loops' own time  111 us (10%)
  local copies, waits for them, and re-layouts  61.9 us (5%)
  matrix products  55.8 us (5%)
  between operations  13.8 us (1%)
  other arithmetic  13.2 us (1%)
    psum x1, waiting for transfers between devices, shards(): lax.psum(local_term, ('row', 'col'))  356 us
    reduce_scatter x1, waiting for transfers between devices, shards(): lax.psum_scatter(summed.reshape(row_tiles * tile_edge, feature_width).ast...  157 us
    all_gather x1, waiting for transfers between devices, shards(): lax.all_gather(features, 'row', axis=0, tiled=True)  144 us
    reduce_scatter x1, waiting for transfers between devices, shards(): lax.psum_scatter(backward_partial.astype(jnp.bfloat16), 'row', scatter_di...  143 us
    all_gather x1, waiting for transfers between devices, shards(): grad_block = lax.all_gather(own_grad, 'col', axis=0, tiled=True)  80.7 us
    another operation x1, loops' own time, shards(): lax.fori_loop(0, live_count, backward_slot, jnp.zeros((col_tiles, tile_ed...  55.4 us
    another operation x1, loops' own time, shards(): lax.fori_loop(0, live_count, forward_slot, jnp.zeros((row_tiles, tile_edg...  55.3 us
    dot_general x12, matrix products, backward_slot(): jnp.einsum('ji,jf->if', tile_block, source, preferred_element_type=jnp.fl...  25.1 us
  transfers between devices with their start and end apart: 5, of which 5 were waited for; matrix products, arithmetic and copies ran while one was open for 6% of the time, Pallas kernels for 0%

commit v1 on v0

v1 whole, which is shorter than its diff:
```python
import functools

import jax
import jax.numpy as jnp
from jax import lax
from jax.experimental import pallas as pl
from jax.experimental.pallas import tpu as pltpu
from jax.sharding import PartitionSpec as P

MESH = pl.DeviceIdType.MESH
F32 = jnp.float32
BF16 = jnp.bfloat16
Z_LO = 3
Z_HI = 4
VMEM_LIMIT = 48 * 1024 * 1024
PART_A, CUT_A, CUT_B = 80, 48, 16


def wrap(value, size):
    return lax.rem(value + 2 * size, size)


def greet(peers):
    barrier = pltpu.get_barrier_semaphore()
    for peer in peers:
        pl.semaphore_signal(barrier, inc=1, device_id=peer, device_id_type=MESH)
    pl.semaphore_wait(barrier, len(peers))


class Links:
    def __init__(self, send, recv):
        self.send, self.recv, self.sent = send, recv, []

    def push(self, src, dst, peer, lands):
        i = len(self.sent)

        def copy(source, target):
            return pltpu.make_async_remote_copy(
                src_ref=source,
                dst_ref=target,
                send_sem=self.send.at[i],
                recv_sem=self.recv.at[i],
                device_id=peer,
                device_id_type=MESH,
            )

        out = copy(src, dst)
        out.start()
        self.sent.append(out)
        return copy(lands, lands).wait_recv

    def drain(self):
        for copy in self.sent:
            copy.wait_send()


def row_place(row):
    return lax.div(row, Z_LO), lax.rem(row, Z_LO)


def row_peers(y, z, rings):
    ups = [{"row": wrap(y + s, rings) * Z_LO + z} for s in (1, -1)]
    sides = [{"row": y * Z_LO + wrap(z + j, Z_LO)} for j in range(1, Z_LO)]
    return ups, sides


def gather_row_kernel(rings, feat_ref, out_ref, buf, send, recv, local):
    row = lax.axis_index("row")
    y, z = row_place(row)
    ups, sides = row_peers(y, z, rings)
    rows = feat_ref.shape[0]
    far = rings // 2
    parts = {"B": (PART_A, rows - PART_A, CUT_B)}
    for j in range(Z_LO):
        parts[j] = (0, PART_A, CUT_A)
    buf[row] = feat_ref[...]
    greet(ups + sides)
    links = Links(send, recv)

    def origin(y_off, z_off):
        return wrap(y + y_off, rings) * Z_LO + wrap(z + z_off, Z_LO)

    def span(tag, sign, hop):
        low, count, cut = parts[tag]
        if hop < far:
            return low, count
        return (low, cut) if sign > 0 else (low + cut, count - cut)

    def ring(tag, sign, hop):
        low, count = span(tag, sign, hop)
        z_off = 0 if tag == "B" else -tag
        mine = buf.at[origin(-sign * (hop - 1), z_off), pl.ds(low, count)]
        theirs = buf.at[origin(-sign * hop, z_off), pl.ds(low, count)]
        return links.push(mine, mine, ups[0 if sign > 0 else 1], theirs)

    def side(y_off, low, count):
        waits = []
        for j in range(1, Z_LO):
            mine = buf.at[origin(y_off, 0), pl.ds(low, count)]
            theirs = buf.at[origin(y_off, -j), pl.ds(low, count)]
            waits.append(links.push(mine, mine, sides[j - 1], theirs))
        return waits

    pending, last = {}, []

    def launch(tag):
        for sign in (1, -1):
            pending[tag, sign] = ring(tag, sign, 1)

    def step(tag, hop):
        for sign in (1, -1):
            pending[tag, sign]()
            if hop < far:
                pending[tag, sign] = ring(tag, sign, hop + 1)
            if tag == "B":
                last.extend(side(-sign * hop, *span(tag, sign, hop)))

    launch("B")
    launch(0)
    low, count, _ = parts[0]
    first = side(0, low, count)
    low, count, _ = parts["B"]
    last.extend(side(0, low, count))
    step("B", 1)
    step(0, 1)
    for j in range(1, Z_LO):
        first[j - 1]()
        launch(j)
    for hop in range(2, far + 1):
        step("B", hop)
        step(0, hop)
        for j in range(1, Z_LO):
            step(j, hop - 1)
    for j in range(1, Z_LO):
        step(j, far)
    for wait in last:
        wait()
    out = pltpu.make_async_copy(buf, out_ref, local)
    out.start()
    links.drain()
    out.wait()


def gather_row(features, n_row):
    rows, width = features.shape
    return pl.pallas_call(
        functools.partial(gather_row_kernel, n_row // Z_LO),
        out_shape=jax.ShapeDtypeStruct((n_row, rows, width), features.dtype),
        in_specs=[pl.BlockSpec(memory_space=pltpu.VMEM)],
        out_specs=pl.BlockSpec(memory_space=pl.ANY),
        scratch_shapes=[
            pltpu.VMEM((n_row, rows, width), features.dtype),
            pltpu.SemaphoreType.DMA((64,)),
            pltpu.SemaphoreType.DMA((64,)),
            pltpu.SemaphoreType.DMA,
        ],
        compiler_params=pltpu.CompilerParams(
            collective_id=0, has_side_effects=True, vmem_limit_bytes=VMEM_LIMIT
        ),
        name="gather_row",
    )(features)


def tiles_kernel(transposed, live, into, origin, tiles, source, out, total):
    total[...] = jnp.zeros_like(total)

    def slot(k, _):
        at = into[k]
        total[at] += lax.dot_general(
            tiles[k],
            source[origin[k]],
            (((0 if transposed else 1,), (0,)), ((), ())),
            preferred_element_type=F32,
        )
        return 0

    lax.fori_loop(0, live[0], slot, 0)
    out[...] = total[...].astype(out.dtype)


def tile_products(tiles, source, live, into, origin, count, transposed):
    edge, width = source.shape[1:]
    smem = pl.BlockSpec(memory_space=pltpu.SMEM)
    vmem = pl.BlockSpec(memory_space=pltpu.VMEM)
    return pl.pallas_call(
        functools.partial(tiles_kernel, transposed),
        out_shape=jax.ShapeDtypeStruct((count, edge, width), BF16),
        in_specs=[smem, smem, smem, vmem, vmem],
        out_specs=vmem,
        scratch_shapes=[pltpu.VMEM((count, edge, width), F32)],
        compiler_params=pltpu.CompilerParams(vmem_limit_bytes=VMEM_LIMIT),
        name="tiles_back" if transposed else "tiles_forward",
    )(live, into, origin, tiles, source)


def layer_kernel(
    n_x,
    part_ref,
    weight_ref,
    cot_ref,
    hidden_ref,
    grads_ref,
    local_ref,
    sums,
    from_core,
    x_far,
    x_near,
    z_sums,
    z_far,
    z_near,
    grads,
    send,
    recv,
    local,
):
    col = lax.axis_index("col")
    core = lax.rem(col, 2)
    chip = lax.div(col, 2)
    x, z = lax.div(chip, Z_HI), lax.rem(chip, Z_HI)
    rows = part_ref.shape[1]
    half = rows // 2

    def place(x_off, z_off, k):
        return (wrap(x + x_off, n_x) * Z_HI + wrap(z + z_off, Z_HI)) * 2 + k

    sibling = {"col": place(0, 0, 1 - core)}
    along_x = {s: {"col": place(s, 0, core)} for s in (1, -1)}
    along_z = {s: {"col": place(0, s, core)} for s in (1, -1)}
    greet([sibling, along_x[1], along_x[-1], along_z[1], along_z[-1]])
    links = Links(send, recv)
    order = (2, 1, -1, 0)
    full = pl.ds(0, rows)
    piece = {1: pl.ds(0, half), -1: pl.ds(half, half)}

    arrived = {}
    for g, z_off in enumerate(order):
        for i, x_off in enumerate(order):
            slot = from_core.at[g, i]
            arrived[g, i] = links.push(part_ref.at[place(x_off, z_off, 1 - core)], slot, sibling, slot)

    def pair_sum(g, i):
        arrived[g, i]()
        mine = part_ref[place(order[i], order[g], core)].astype(F32)
        sums[g, i] = (mine + from_core[g, i].astype(F32)).astype(BF16)

    def add(target, at, other):
        target[at] = (target[at].astype(F32) + other.astype(F32)).astype(BF16)

    waits = {}

    def x_first(g):
        pair_sum(g, 0)
        for n, s in enumerate((1, -1)):
            slot = x_far.at[g, n]
            waits[g, "far", s] = links.push(sums.at[g, 0, piece[s]], slot, along_x[s], slot)

    def x_second(g):
        for n, s in enumerate((1, -1)):
            pair_sum(g, 1 + n)
            waits[g, "far", s]()
            add(sums, (g, 1 + n, piece[s]), x_far[g, n])
            slot = x_near.at[g, n]
            waits[g, "near", s] = links.push(sums.at[g, 1 + n], slot, along_x[s], slot)

    def x_last(g):
        pair_sum(g, 3)
        for s in (1, -1):
            waits[g, "near", s]()
        total = sums[g, 3].astype(F32) + x_near[g, 0].astype(F32) + x_near[g, 1].astype(F32)
        z_sums[g] = total.astype(BF16)

    z_waits = {}

    def z_first():
        for n, s in enumerate((1, -1)):
            slot = z_far.at[n]
            z_waits["far", s] = links.push(z_sums.at[0, piece[s]], slot, along_z[s], slot)

    def z_second(g):
        n, s = g - 1, order[g]
        z_waits["far", s]()
        add(z_sums, (g, piece[s]), z_far[n])
        slot = z_near.at[n]
        z_waits["near", s] = links.push(z_sums.at[g], slot, along_z[s], slot)

    x_first(0)
    x_first(1)
    x_second(0)
    x_first(2)
    x_second(1)
    x_last(0)
    z_first()
    x_first(3)
    x_second(2)
    x_last(1)
    z_second(1)
    x_second(3)
    x_last(2)
    z_second(2)
    x_last(3)
    for s in (1, -1):
        z_waits["near", s]()
    total = z_sums[3].astype(F32) + z_near[0].astype(F32) + z_near[1].astype(F32)
    own_sum = total.astype(BF16)

    pre_act = jnp.dot(own_sum, weight_ref[...], preferred_element_type=F32)
    gate = jax.nn.sigmoid(pre_act)
    own_grad = (cot_ref[...].astype(F32) * gate * (1.0 + pre_act * (1.0 - gate))).astype(BF16)
    grads[col] = own_grad

    last = []

    def chunk(x_off, z_off, k, where):
        return grads.at[place(x_off, z_off, k), where]

    def to_core(x_off, z_off, where):
        mine = chunk(x_off, z_off, core, where)
        last.append(links.push(mine, mine, sibling, chunk(x_off, z_off, 1 - core, where)))

    def to_z(s, z_off, where):
        mine = chunk(0, z_off, core, where)
        return links.push(mine, mine, along_z[s], chunk(0, z_off - s, core, where))

    def to_x(s, x_off, z_off, where):
        mine = chunk(x_off, z_off, core, where)
        return links.push(mine, mine, along_x[s], chunk(x_off - s, z_off, core, where))

    def cut(where):
        size = where.size // 2
        return {1: pl.ds(where.start, size), -1: pl.ds(where.start + size, size)}

    def x_start(z_off, where):
        return {s: to_x(s, 0, z_off, where) for s in (1, -1)}

    def x_pass(near, z_off, where):
        far = {}
        for s in (1, -1):
            near[s]()
            far[s] = to_x(s, -s, z_off, cut(where)[s])
            to_core(-s, z_off, where)
        return far

    def x_end(far, z_off, where):
        for s in (1, -1):
            far[s]()
            to_core(2, z_off, cut(where)[s])

    near_z = {s: to_z(s, 0, full) for s in (1, -1)}
    near = [x_start(0, full)]
    to_core(0, 0, full)
    hidden_ref[...] = (pre_act * gate).astype(hidden_ref.dtype)
    local_ref[...] = lax.dot_general(
        own_sum, own_grad, (((0,), (0,)), ((), ())), preferred_element_type=F32
    )
    far_z = {}
    for s in (1, -1):
        near_z[s]()
        far_z[s] = to_z(s, -s, piece[s])
        near.append(x_start(-s, full))
        to_core(0, -s, full)
    far = [x_pass(near[0], 0, full)]
    for s in (1, -1):
        far_z[s]()
        near.append(x_start(2, piece[s]))
        to_core(0, 2, piece[s])
    spans = [(0, full), (-1, full), (1, full), (2, piece[1]), (2, piece[-1])]
    for i in range(1, 5):
        far.append(x_pass(near[i], *spans[i]))
        x_end(far[i - 1], *spans[i - 1])
    x_end(far[4], *spans[4])
    for wait in last:
        wait()
    out = pltpu.make_async_copy(grads, grads_ref, local)
    out.start()
    links.drain()
    out.wait()


def layer(partial, weight, cotangent, n_col):
    _, rows, width = partial.shape
    vmem = pl.BlockSpec(memory_space=pltpu.VMEM)
    return pl.pallas_call(
        functools.partial(layer_kernel, n_col // (2 * Z_HI)),
        out_shape=(
            jax.ShapeDtypeStruct((rows, width), BF16),
            jax.ShapeDtypeStruct((n_col, rows, width), BF16),
            jax.ShapeDtypeStruct((width, width), F32),
        ),
        in_specs=[vmem, vmem, vmem],
        out_specs=(vmem, pl.BlockSpec(memory_space=pl.ANY), vmem),
        scratch_shapes=[
            pltpu.VMEM((4, 4, rows, width), BF16),
            pltpu.VMEM((4, 4, rows, width), BF16),
            pltpu.VMEM((4, 2, rows // 2, width), BF16),
            pltpu.VMEM((4, 2, rows, width), BF16),
            pltpu.VMEM((4, rows, width), BF16),
            pltpu.VMEM((2, rows // 2, width), BF16),
            pltpu.VMEM((2, rows, width), BF16),
            pltpu.VMEM((n_col, rows, width), BF16),
            pltpu.SemaphoreType.DMA((96,)),
            pltpu.SemaphoreType.DMA((96,)),
            pltpu.SemaphoreType.DMA,
        ],
        compiler_params=pltpu.CompilerParams(
            collective_id=1, has_side_effects=True, vmem_limit_bytes=VMEM_LIMIT
        ),
        name="layer",
    )(partial, weight, cotangent)


def finish_kernel(
    rings,
    n_x,
    scale,
    part_ref,
    weight_ref,
    local_ref,
    out_ref,
    gw_ref,
    a_in,
    a_sum,
    a_side,
    b_in,
    b_sum,
    b_side,
    w_core,
    w_x,
    w_y,
    w_lo,
    w_hi,
    w_piece,
    w_sum,
    send,
    recv,
):
    row, col = lax.axis_index("row"), lax.axis_index("col")
    y, z = row_place(row)
    core = lax.rem(col, 2)
    chip = lax.div(col, 2)
    x, z_hi = lax.div(chip, Z_HI), lax.rem(chip, Z_HI)
    rows = part_ref.shape[1]
    far = rings // 2
    ups, sides = row_peers(y, z, rings)
    up = {1: ups[0], -1: ups[1]}
    sibling = {"col": chip * 2 + 1 - core}
    x_peers = [{"col": (wrap(x + j, n_x) * Z_HI + z_hi) * 2 + core} for j in range(1, n_x)]
    y_peers = [{"row": wrap(y + j, rings) * Z_LO + z} for j in range(1, rings)]
    hi_peers = [{"col": (x * Z_HI + wrap(z_hi + j, Z_HI)) * 2 + core} for j in range(1, Z_HI)]
    greet([sibling] + x_peers + y_peers + sides + hi_peers)
    links = Links(send, recv)

    def dest(y_off, z_off):
        return wrap(y + y_off, rings) * Z_LO + wrap(z + z_off, Z_LO)

    depth = local_ref.shape[0]
    n_pair, n_quarter, n_piece = depth // 2, depth // 2 // n_x, depth // 2 // n_x // rings

    def stage_core():
        return [
            links.push(local_ref.at[pl.ds((1 - core) * n_pair, n_pair)], w_core, sibling, w_core)
        ]

    def stage_x():
        w_sum[...] = local_ref[pl.ds(core * n_pair, n_pair)] + w_core[...]
        return [
            links.push(w_sum.at[pl.ds(wrap(x + j, n_x) * n_quarter, n_quarter)], w_x.at[j - 1], x_peers[j - 1], w_x.at[j - 1])
            for j in range(1, n_x)
        ]

    def stage_y():
        mine = pl.ds(x * n_quarter, n_quarter)
        total = w_sum[mine]
        for j in range(1, n_x):
            total += w_x[j - 1]
        w_sum[mine] = total
        return [
            links.push(
                w_sum.at[pl.ds(x * n_quarter + wrap(y + j, rings) * n_piece, n_piece)],
                w_y.at[j - 1],
                y_peers[j - 1],
                w_y.at[j - 1],
            )
            for j in range(1, rings)
        ]

    def stage_lo():
        total = w_sum[pl.ds(x * n_quarter + y * n_piece, n_piece)]
        for j in range(1, rings):
            total += w_y[j - 1]
        w_piece[0] = total
        return [links.push(w_piece.at[0], w_lo.at[j - 1], sides[j - 1], w_lo.at[j - 1]) for j in range(1, Z_LO)]

    def stage_hi():
        total = w_piece[0]
        for j in range(1, Z_LO):
            total += w_lo[j - 1]
        w_piece[1] = total
        return [links.push(w_piece.at[1], w_hi.at[j - 1], hi_peers[j - 1], w_hi.at[j - 1]) for j in range(1, Z_HI)]

    def back(y_off, x_off, k, count):
        base = k * n_pair + wrap(x + x_off, n_x) * n_quarter + wrap(y + y_off, rings) * n_piece
        return gw_ref.at[pl.ds(base, count)]

    def stage_back_y():
        total = w_piece[1]
        for j in range(1, Z_HI):
            total += w_hi[j - 1]
        gw_ref[pl.ds(core * n_pair + x * n_quarter + y * n_piece, n_piece)] = total * scale
        mine = back(0, 0, core, n_piece)
        return [links.push(mine, mine, y_peers[j - 1], back(-j, 0, core, n_piece)) for j in range(1, rings)]

    def quarter(x_off, k):
        return gw_ref.at[pl.ds(k * n_pair + wrap(x + x_off, n_x) * n_quarter, n_quarter)]

    def stage_back_x():
        mine = quarter(0, core)
        return [links.push(mine, mine, x_peers[j - 1], quarter(-j, core)) for j in range(1, n_x)]

    def stage_back_core():
        mine = gw_ref.at[pl.ds(core * n_pair, n_pair)]
        return [links.push(mine, mine, sibling, gw_ref.at[pl.ds((1 - core) * n_pair, n_pair)])]

    stages = [stage_core, stage_x, stage_y, stage_lo, stage_hi, stage_back_y, stage_back_x, stage_back_core]
    weight_waits = []

    def weight_step():
        for wait in weight_waits:
            wait()
        del weight_waits[:]
        if stages:
            weight_waits.extend(stages.pop(0)())

    waits = {}

    def half(low, count, cut, sign):
        return pl.ds(low, cut) if sign > 0 else pl.ds(low + cut, count - cut)

    def a_send(j, hop):
        for n, s in enumerate((1, -1)):
            at = a_sum.at[j, n, hop - 1]
            slot = a_in.at[j, n, hop - 1]
            if hop == far:
                where = half(0, PART_A, CUT_A, s)
                a_sum[j, n, hop - 1, where] = part_ref[dest(s * hop, j), where]
                at, slot = at.at[where], slot.at[where]
            else:
                mine = part_ref[dest(s * hop, j), pl.ds(0, PART_A)]
                waits["A", j, s]()
                if hop + 1 == far:
                    a_sum[j, n, hop - 1] = mine
                    where = half(0, PART_A, CUT_A, s)
                    both = a_sum[j, n, hop - 1, where].astype(F32) + a_in[j, n, hop, where].astype(F32)
                    a_sum[j, n, hop - 1, where] = both.astype(BF16)
                else:
                    a_sum[j, n, hop - 1] = (mine.astype(F32) + a_in[j, n, hop].astype(F32)).astype(BF16)
            waits["A", j, s] = links.push(at, slot, up[s], slot)

    def a_total(j):
        for s in (1, -1):
            waits["A", j, s]()
        mine = part_ref[dest(0, j), pl.ds(0, PART_A)].astype(F32)
        return mine + a_in[j, 0, 0].astype(F32) + a_in[j, 1, 0].astype(F32)

    side_waits = []

    def a_across(j):
        a_side[0, j - 1] = a_total(j).astype(BF16)
        slot = a_side.at[1, j - 1]
        side_waits.append(links.push(a_side.at[0, j - 1], slot, sides[j - 1], slot))

    n_b = rows - PART_A
    part_b = pl.ds(PART_A, n_b)
    offsets = [far] + [s * h for h in range(far - 1, 0, -1) for s in (1, -1)] + [0]
    b_waits = {}

    def b_across():
        for i, y_off in enumerate(offsets):
            b_waits[y_off] = []
            for j in range(1, Z_LO):
                slot = b_side.at[i, j - 1]
                b_waits[y_off].append(
                    links.push(part_ref.at[dest(y_off, j), part_b], slot, sides[j - 1], slot)
                )

    def b_total(y_off):
        i = offsets.index(y_off)
        for wait in b_waits[y_off]:
            wait()
        mine = part_ref[dest(y_off, 0), part_b].astype(F32)
        return mine + b_side[i, 0].astype(F32) + b_side[i, 1].astype(F32)

    def b_send(hop):
        if hop == far:
            b_sum[0, far - 1] = b_total(far).astype(BF16)
        for n, s in enumerate((1, -1)):
            if hop == far:
                where = half(0, n_b, CUT_B, s)
                at, slot = b_sum.at[0, hop - 1, where], b_in.at[n, hop - 1, where]
            else:
                total = b_total(s * hop)
                at, slot = b_sum.at[n, hop - 1], b_in.at[n, hop - 1]
                waits["B", s]()
                if hop + 1 == far:
                    where = half(0, n_b, CUT_B, s)
                    b_sum[n, hop - 1] = total.astype(BF16)
                    both = b_sum[n, hop - 1, where].astype(F32) + b_in[n, hop, where].astype(F32)
                    b_sum[n, hop - 1, where] = both.astype(BF16)
                else:
                    b_sum[n, hop - 1] = (total + b_in[n, hop].astype(F32)).astype(BF16)
            waits["B", s] = links.push(at, slot, up[s], slot)

    for j in (1, 2, 0):
        a_send(j, far)
    b_across()
    weight_step()
    for hop in range(far - 1, 0, -1):
        for j in (1, 2):
            a_send(j, hop)
        weight_step()
        b_send(hop + 1)
        a_send(0, hop)
        weight_step()
    for j in (1, 2):
        a_across(j)
    b_send(1)
    weight_step()
    total_a = a_total(0)
    total_b = b_total(0)
    for s in (1, -1):
        waits["B", s]()
    total_b += b_in[0, 0].astype(F32) + b_in[1, 0].astype(F32)
    for j, wait in enumerate(side_waits):
        wait()
        total_a += a_side[1, j].astype(F32)
    for where, total in ((pl.ds(0, PART_A), total_a), (part_b, total_b)):
        out_ref[where] = lax.dot_general(
            total.astype(BF16), weight_ref[...], (((1,), (1,)), ((), ())), preferred_element_type=F32
        ).astype(out_ref.dtype)
    while stages or weight_waits:
        weight_step()
    links.drain()


def finish(partial, weight, local, n_row, n_col, scale):
    _, rows, width = partial.shape
    rings, n_x = n_row // Z_LO, n_col // (2 * Z_HI)
    far, n_b = rings // 2, rows - PART_A
    depth = width // 2
    vmem = pl.BlockSpec(memory_space=pltpu.VMEM)
    return pl.pallas_call(
        functools.partial(finish_kernel, rings, n_x, scale),
        out_shape=(
            jax.ShapeDtypeStruct((rows, width), BF16),
            jax.ShapeDtypeStruct((width, width), F32),
        ),
        in_specs=[vmem, vmem, vmem],
        out_specs=(vmem, vmem),
        scratch_shapes=[
            pltpu.VMEM((Z_LO, 2, far, PART_A, width), BF16),
            pltpu.VMEM((Z_LO, 2, far, PART_A, width), BF16),
            pltpu.VMEM((2, Z_LO - 1, PART_A, width), BF16),
            pltpu.VMEM((2, far, n_b, width), BF16),
            pltpu.VMEM((2, far, n_b, width), BF16),
            pltpu.VMEM((rings, Z_LO - 1, n_b, width), BF16),
            pltpu.VMEM((depth, width), F32),
            pltpu.VMEM((n_x - 1, depth // n_x, width), F32),
            pltpu.VMEM((rings - 1, depth // n_x // rings, width), F32),
            pltpu.VMEM((Z_LO - 1, depth // n_x // rings, width), F32),
            pltpu.VMEM((Z_HI - 1, depth // n_x // rings, width), F32),
            pltpu.VMEM((2, depth // n_x // rings, width), F32),
            pltpu.VMEM((depth, width), F32),
            pltpu.SemaphoreType.DMA((128,)),
            pltpu.SemaphoreType.DMA((128,)),
        ],
        compiler_params=pltpu.CompilerParams(
            collective_id=2, has_side_effects=True, vmem_limit_bytes=VMEM_LIMIT
        ),
        name="finish",
    )(partial, weight, local)


def shards(features, tile_values, tile_rows, tile_cols, tile_live, weight, cotangent):
    rows, width = features.shape
    edge = tile_values.shape[1]
    n_row, n_col = lax.axis_size("row"), lax.axis_size("col")
    row_tiles, col_tiles = rows * n_col // edge, rows * n_row // edge
    column_block = gather_row(features, n_row).reshape(col_tiles, edge, width)
    partial = tile_products(
        tile_values, column_block, tile_live, tile_rows, tile_cols, row_tiles, False
    )
    hidden, grads, local = layer(partial.reshape(n_col, rows, width), weight, cotangent, n_col)
    back = tile_products(
        tile_values,
        grads.reshape(row_tiles, edge, width),
        tile_live,
        tile_cols,
        tile_rows,
        col_tiles,
        True,
    )
    scale = float(rows * n_row * n_col) ** -0.5
    grad_features, grad_weight = finish(
        back.reshape(n_row, rows, width), weight, local, n_row, n_col, scale
    )
    return hidden, grad_features, grad_weight


def solution(mesh):
    return jax.shard_map(
        shards,
        mesh=mesh,
        in_specs=(
            P(("col", "row"), None),
            P(("row", "col"), None, None),
            P(("row", "col")),
            P(("row", "col")),
            P(("row", "col")),
            P(),
            P(("row", "col"), None),
        ),
        out_specs=(P(("row", "col"), None), P(("col", "row"), None), P()),
        check_vma=False,
    )
```

time: 1140 us -> 184 us (0.16)
  the two profiles are of different devices: /device:TPU:198 before, /device:TPU:1 now
where the time goes in v1:
time: 184 us
  Pallas kernels  177 us (96%)
  local copies, waits for them, and re-layouts  5.13 us (3%)
    pallas_call x1, Pallas kernels, layer(): pl.pallas_call(functools.partial(layer_kernel, n_col // (2 * Z_HI)), out_...  81.4 us
    pallas_call x1, Pallas kernels, finish(): pl.pallas_call(functools.partial(finish_kernel, rings, n_x, scale), out_s...  52.2 us
    pallas_call x1, Pallas kernels, gather_row(): pl.pallas_call(functools.partial(gather_row_kernel, n_row // Z_LO), out_s...  33.2 us
    pallas_call x2, Pallas kernels, tile_products(): pl.pallas_call(functools.partial(tiles_kernel, transposed), out_shape=jax...  10.7 us
    unnamed x17, local copies, waits for them, and re-layouts  5.13 us

profile of v1, /device:TPU:1, one launch (start us, length us, event | category | flops | bytes accessed | tf_op | source)
XLA Modules:
  0.0 184.1 jit_solution(13324351764433478680)
XLA Ops:
  0.6 0.0 copy-start
  1.4 0.0 copy-start.3
  1.4 0.9 copy-done.3
  2.3 0.0 copy-start.5
  2.3 0.0 copy-start.6
  2.3 33.2 %gather_row.1 = bf16[24,128,512]{2,1,0:T(8,128)(2,1)S(1)} custom-call(bf16[128,512]{1,0:T(8,128)(2,1)S(1)} %copy-done.3), custom_call_target="tpu_custom_call" | custom-call | tf_op jit(solution)/shard_map/gather_row/pallas_call | solution.py:146
  35.5 0.0 copy-done
  35.5 0.0 copy-done.5
  35.5 0.0 copy-done.6
  35.5 0.0 copy-start.2
  35.6 0.0 copy-start.4
  35.6 5.5 %tiles_forward.1 = bf16[16,256,512]{2,1,0:T(8,128)(2,1)} custom-call(s32[1]{0:T(128)S(6)} %copy.13.live, s32[16]{0:T(128)S(1)} %copy-done.5, s32[16]{0:T(128)S(1)} %copy-done.6, bf16[16,256,256]{2,1,0:T(8,128)(2,1)S(1)} %copy-done, bf16[12,256,512]{2,1,0:T(8,128)(2,1)S(1)} %bitcast.5), custom_call_target="tpu_custom_call" | custom-call | tf_op jit(solution)/shard_map/tiles_forward/pallas_call | solution.py:185
  41.1 0.0 copy-done.2
  41.1 0.0 copy-done.4
  41.1 81.4 %layer.1 = (bf16[128,512]{1,0:T(8,128)(2,1)S(1)}, bf16[32,128,512]{2,1,0:T(8,128)(2,1)S(1)}, f32[512,512]{1,0:T(8,128)S(1)}) custom-call(bf16[32,128,512]{2,1,0:T(8,128)(2,1)} %bitcast.7, bf16[512,512]{1,0:T(8,128)(2,1)S(1)} %copy-done.2, bf16[128,512]{1,0:T(8,128)(2,1)S(1)} %copy-done.4), custom_call_target="tpu_custom_call" | custom-call | tf_op jit(solution)/shard_map/layer/pallas_call | solution.py:382
  122.5 0.0 copy-start.1
  122.5 1.9 %copy-done.1 = bf16[32,128,512]{2,1,0:T(8,128)(2,1)} copy-done((bf16[32,128,512]{2,1,0:T(8,128)(2,1)}, bf16[32,128,512]{2,1,0:T(8,128)(2,1)S(1)}, u32[]{:S(2)}) %copy-start.1) | copy-done | bytes 4194328
  124.4 5.2 %tiles_back.1 = bf16[12,256,512]{2,1,0:T(8,128)(2,1)S(1)} custom-call(s32[1]{0:T(128)S(6)} %copy.13.live, s32[16]{0:T(128)S(1)} %copy-done.6, s32[16]{0:T(128)S(1)} %copy-done.5, bf16[16,256,256]{2,1,0:T(8,128)(2,1)S(1)} %copy-done, bf16[16,256,512]{2,1,0:T(8,128)(2,1)} %bitcast.6), custom_call_target="tpu_custom_call" | custom-call | tf_op jit(solution)/shard_map/tiles_back/pallas_call | solution.py:185
  129.6 52.2 %finish.1 = (bf16[128,512]{1,0:T(8,128)(2,1)S(1)}, f32[512,512]{1,0:T(8,128)S(1)}) custom-call(bf16[24,128,512]{2,1,0:T(8,128)(2,1)S(1)} %bitcast.4, bf16[512,512]{1,0:T(8,128)(2,1)S(1)} %copy-done.2, f32[512,512]{1,0:T(8,128)S(1)} %get-tuple-element.10.local_ref), custom_call_target="tpu_custom_call" | custom-call | tf_op jit(solution)/shard_map/finish/pallas_call | solution.py:650
  181.8 0.7 copy.14
  182.4 0.7 copy.15
  183.1 1.0 copy.16
Async XLA Ops:
  0.6 34.9 %copy-start = (bf16[16,256,256]{2,1,0:T(8,128)(2,1)S(1)}, bf16[16,256,256]{2,1,0:T(8,128)(2,1)}, u32[]{:S(2)}) copy-start(bf16[16,256,256]{2,1,0:T(8,128)(2,1)} %tiles.3) | copy-start | bytes 6291460
  1.4 0.9 copy-start.3
  2.3 33.2 %copy-start.5 = (s32[16]{0:T(128)S(1)}, s32[16]{0:T(128)}, u32[]{:S(2)}) copy-start(s32[16]{0:T(128)} %origin.3) | copy-start | bytes 196
  2.3 33.2 %copy-start.6 = (s32[16]{0:T(128)S(1)}, s32[16]{0:T(128)}, u32[]{:S(2)}) copy-start(s32[16]{0:T(128)} %into.3) | copy-start | bytes 196
  35.5 5.5 %copy-start.2 = (bf16[512,512]{1,0:T(8,128)(2,1)S(1)}, bf16[512,512]{1,0:T(8,128)(2,1)}, u32[]{:S(2)}) copy-start(bf16[512,512]{1,0:T(8,128)(2,1)} %weight_ref.3) | copy-start | bytes 1572868
  35.6 5.5 %copy-start.4 = (bf16[128,512]{1,0:T(8,128)(2,1)S(1)}, bf16[128,512]{1,0:T(8,128)(2,1)}, u32[]{:S(2)}) copy-start(bf16[128,512]{1,0:T(8,128)(2,1)} %cot_ref.1) | copy-start | bytes 393220
  122.5 1.9 %copy-start.1 = (bf16[32,128,512]{2,1,0:T(8,128)(2,1)}, bf16[32,128,512]{2,1,0:T(8,128)(2,1)S(1)}, u32[]{:S(2)}) copy-start(bf16[32,128,512]{2,1,0:T(8,128)(2,1)S(1)} %get-tuple-element.9) | copy-start | bytes 12582916

commit v2 on v0

v2 whole, which is shorter than its diff:
```python
import functools

import jax
import jax.numpy as jnp
from jax import lax
from jax.experimental import pallas as pl
from jax.experimental.pallas import tpu as pltpu
from jax.sharding import PartitionSpec as P

MESH = pl.DeviceIdType.MESH
F32 = jnp.float32
BF16 = jnp.bfloat16
Z_LO = 3
Z_HI = 4
VMEM_LIMIT = 58 * 1024 * 1024
GATHER_PART, GATHER_CUTS = 64, (32, 32)
SUM_PART, SUM_CUTS = 80, (48, 16)


def wrap(value, size):
    return lax.rem(value + 2 * size, size)


class Links:
    def __init__(self, send, recv):
        self.send, self.recv, self.count, self.sent = send, recv, 0, []

    def push(self, src, dst, peer, lands):
        i = self.count
        self.count += 1

        def copy(source, target):
            return pltpu.make_async_remote_copy(
                src_ref=source,
                dst_ref=target,
                send_sem=self.send.at[i],
                recv_sem=self.recv.at[i],
                device_id=peer,
                device_id_type=MESH,
            )

        out = copy(src, dst)
        out.start()
        self.sent.append(out)
        return copy(lands, lands).wait_recv

    def drain(self):
        for copy in self.sent:
            copy.wait_send()
        self.sent = []


class Place:
    def __init__(self, rings, n_x):
        self.rings, self.n_x = rings, n_x
        self.row, self.col = lax.axis_index("row"), lax.axis_index("col")
        self.y, self.zl = lax.div(self.row, Z_LO), lax.rem(self.row, Z_LO)
        self.chip, self.core = lax.div(self.col, 2), lax.rem(self.col, 2)
        self.x, self.zh = lax.div(self.chip, Z_HI), lax.rem(self.chip, Z_HI)
        self.sibling = {"col": self.chip * 2 + 1 - self.core}
        self.xs = {j: {"col": self.chip_at(j, 0) * 2 + self.core} for j in range(1, n_x)}
        self.zhs = {j: {"col": self.chip_at(0, j) * 2 + self.core} for j in range(1, Z_HI)}
        self.ys = {j: {"row": self.row_at(j, 0)} for j in range(1, rings)}
        self.zls = {j: {"row": self.row_at(0, j)} for j in range(1, Z_LO)}
        for peers, size in ((self.xs, n_x), (self.zhs, Z_HI), (self.ys, rings), (self.zls, Z_LO)):
            peers[-1] = peers[size - 1]

    def chip_at(self, x_off, z_off):
        return wrap(self.x + x_off, self.n_x) * Z_HI + wrap(self.zh + z_off, Z_HI)

    def row_at(self, y_off, z_off):
        return wrap(self.y + y_off, self.rings) * Z_LO + wrap(self.zl + z_off, Z_LO)

    def greet(self):
        barrier = pltpu.get_barrier_semaphore()
        peers = [self.sibling]
        for group in (self.xs, self.zhs, self.ys, self.zls):
            peers += [peer for j, peer in group.items() if j > 0]
        for peer in peers:
            pl.semaphore_signal(barrier, inc=1, device_id=peer, device_id_type=MESH)
        pl.semaphore_wait(barrier, len(peers))


def chunk(ref, index, rows=None):
    at = ref.at[lax.div(index, 2), lax.rem(index, 2)]
    return at if rows is None else at.at[rows]


def gather_row(here, links, buf):
    rows = buf.shape[2]
    far = here.rings // 2
    parts = {"B": (GATHER_PART, rows - GATHER_PART, GATHER_CUTS[1])}
    for j in range(Z_LO):
        parts[j] = (0, GATHER_PART, GATHER_CUTS[0])

    def span(tag, sign, hop):
        low, count, cut = parts[tag]
        if hop < far:
            return pl.ds(low, count)
        return pl.ds(low, cut) if sign > 0 else pl.ds(low + cut, count - cut)

    def ring(tag, sign, hop):
        where = span(tag, sign, hop)
        z_off = 0 if tag == "B" else -tag
        mine = chunk(buf, here.row_at(-sign * (hop - 1), z_off), where)
        theirs = chunk(buf, here.row_at(-sign * hop, z_off), where)
        return links.push(mine, mine, here.ys[sign], theirs)

    def side(y_off, where):
        waits = []
        for j in range(1, Z_LO):
            mine = chunk(buf, here.row_at(y_off, 0), where)
            theirs = chunk(buf, here.row_at(y_off, -j), where)
            waits.append(links.push(mine, mine, here.zls[j], theirs))
        return waits

    pending, last = {}, []

    def launch(tag):
        for sign in (1, -1):
            pending[tag, sign] = ring(tag, sign, 1)

    def step(tag, hop):
        for sign in (1, -1):
            pending[tag, sign]()
            if hop < far:
                pending[tag, sign] = ring(tag, sign, hop + 1)
            if tag == "B":
                last.extend(side(-sign * hop, span(tag, sign, hop)))

    launch("B")
    launch(0)
    first = side(0, span(0, 1, 1))
    last.extend(side(0, span("B", 1, 1)))
    step("B", 1)
    step(0, 1)
    for j in range(1, Z_LO):
        first[j - 1]()
        launch(j)
    for hop in range(2, far + 1):
        step("B", hop)
        step(0, hop)
        for j in range(1, Z_LO):
            step(j, hop - 1)
    for j in range(1, Z_LO):
        step(j, far)
    for wait in last:
        wait()


def tile_products(tiles, source, into, origin, total, transposed):
    slots = tiles.shape[0]
    total[slots] = jnp.zeros(total.shape[1:], F32)

    def slot(k, _):
        before = jnp.int32(slots)
        for j in range(slots):
            before = jnp.where((j < k) & (into[j] == into[k]), j, before)
        block = source[origin[k]]
        total[k] = total[before] + lax.dot_general(
            tiles[k],
            block.reshape(block.shape[0] * block.shape[1], block.shape[2]),
            (((0 if transposed else 1,), (0,)), ((), ())),
            preferred_element_type=F32,
        )
        return 0

    lax.fori_loop(0, slots, slot, 0)


def target_sum(total, into, live, target):
    slots = total.shape[0] - 1
    count = live[0]
    last = jnp.int32(slots)
    for j in range(slots):
        last = jnp.where((j < count) & (into[j] == target), j, last)
    return total[last]


ORDER = (2, 1, -1, 0)


def sum_col(here, links, tile, part, from_core, sums, x_far, x_near, z_sums, z_far, z_near):
    rows, width = part.shape[2:]
    half, quarter = rows // 2, rows // 4
    halves = (pl.ds(0, half), pl.ds(half, half))
    core = here.core
    arrived = {}
    for g, z_off in enumerate(ORDER):
        for i, x_off in enumerate(ORDER):
            chip = here.chip_at(x_off, z_off)
            part[chip] = tile(chip).astype(BF16).reshape(2, rows, width)
            slot = from_core.at[g, i]
            arrived[g, i] = links.push(part.at[chip, 1 - core], slot, here.sibling, slot)

    def pair_sum(g, i):
        if (g, i) in arrived:
            arrived.pop((g, i))()
            sums[g, i] = part[here.chip_at(ORDER[i], ORDER[g]), core] + from_core[g, i]

    def quarter_of(h, s):
        return pl.ds(h * half + (0 if s > 0 else quarter), quarter)

    waits = {}

    def x_first(b):
        g, h = b
        pair_sum(g, 0)
        for n, s in enumerate((1, -1)):
            slot = x_far.at[g, h, n]
            waits[b, "far", s] = links.push(sums.at[g, 0, quarter_of(h, s)], slot, here.xs[s], slot)

    def x_second(b):
        g, h = b
        for n, s in enumerate((1, -1)):
            pair_sum(g, 1 + n)
            waits[b, "far", s]()
            where = quarter_of(h, s)
            sums[g, 1 + n, where] = sums[g, 1 + n, where] + x_far[g, h, n]
            slot = x_near.at[g, h, n]
            waits[b, "near", s] = links.push(sums.at[g, 1 + n, halves[h]], slot, here.xs[s], slot)

    def x_last(b):
        g, h = b
        pair_sum(g, 3)
        for s in (1, -1):
            waits[b, "near", s]()
        total = sums[g, 3, halves[h]].astype(F32) + x_near[g, h, 0].astype(F32) + x_near[g, h, 1].astype(F32)
        z_sums[g, halves[h]] = total.astype(BF16)
        if g == 0:
            n, s = h, (1, -1)[h]
            slot = z_far.at[n]
            waits["z_far", s] = links.push(z_sums.at[g, halves[h]], slot, here.zhs[s], slot)
        elif g < 3:
            n, s = g - 1, ORDER[g]
            if h == n:
                waits["z_far", s]()
                z_sums[g, halves[h]] = z_sums[g, halves[h]] + z_far[n]
            slot = z_near.at[n, halves[h]]
            waits["z_near", s, h] = links.push(z_sums.at[g, halves[h]], slot, here.zhs[s], slot)

    blocks = [(0, 0), (0, 1), (1, 1), (2, 0), (1, 0), (2, 1), (3, 0), (3, 1)]
    x_first(blocks[0])
    x_first(blocks[1])
    for n, b in enumerate(blocks):
        x_second(b)
        if n + 2 < len(blocks):
            x_first(blocks[n + 2])
        if n >= 1:
            x_last(blocks[n - 1])
    x_last(blocks[-1])
    links.drain()
    for s, h in ((1, 1), (-1, 0), (1, 0), (-1, 1)):
        waits["z_near", s, h]()
    total = z_sums[3].astype(F32) + z_near[0].astype(F32) + z_near[1].astype(F32)
    return total.astype(BF16)


def gather_col(here, links, grads, between):
    rows = grads.shape[2]
    half = rows // 2
    piece = {1: pl.ds(0, half), -1: pl.ds(half, half)}
    last = []

    def at(x_off, z_off, k, where):
        return grads.at[here.chip_at(x_off, z_off), k, where]

    def to_core(x_off, z_off, where):
        mine = at(x_off, z_off, here.core, where)
        last.append(links.push(mine, mine, here.sibling, at(x_off, z_off, 1 - here.core, where)))

    def to_z(s, z_off, where):
        mine = at(0, z_off, here.core, where)
        return links.push(mine, mine, here.zhs[s], at(0, z_off - s, here.core, where))

    def to_x(s, x_off, z_off, where):
        mine = at(x_off, z_off, here.core, where)
        return links.push(mine, mine, here.xs[s], at(x_off - s, z_off, here.core, where))

    def cut(where):
        size = where.size // 2
        return {1: pl.ds(where.start, size), -1: pl.ds(where.start + size, size)}

    near, far = {}, {}

    def x_start(z_off, side):
        near[z_off, side] = {s: to_x(s, 0, z_off, piece[side]) for s in (1, -1)}

    def x_pass(z_off, side):
        far[z_off, side] = {}
        for s in (1, -1):
            near[z_off, side][s]()
            far[z_off, side][s] = to_x(s, -s, z_off, cut(piece[side])[s])
            to_core(-s, z_off, piece[side])

    def x_end(z_off, side):
        for s in (1, -1):
            far[z_off, side][s]()
            to_core(2, z_off, cut(piece[side])[s])

    first = {s: to_z(s, 0, piece[s]) for s in (1, -1)}
    second = {s: to_z(s, 0, piece[-s]) for s in (1, -1)}
    x_start(0, 1)
    x_start(0, -1)
    to_core(0, 0, pl.ds(0, rows))
    between()
    x_pass(0, 1)
    x_pass(0, -1)
    between()
    opposite = {}
    for s in (1, -1):
        first[s]()
        opposite[s] = to_z(s, -s, piece[s])
        x_start(-s, s)
        to_core(0, -s, piece[s])
    x_end(0, 1)
    x_end(0, -1)
    for s in (1, -1):
        x_pass(-s, s)
    for s in (1, -1):
        second[s]()
        x_start(-s, -s)
        to_core(0, -s, piece[-s])
    for s in (1, -1):
        x_end(-s, s)
    between()
    for s in (1, -1):
        x_pass(-s, -s)
    for s in (1, -1):
        opposite[s]()
        x_start(2, s)
        to_core(0, 2, piece[s])
    for s in (1, -1):
        x_end(-s, -s)
    between()
    for s in (1, -1):
        x_pass(2, s)
    for s in (1, -1):
        x_end(2, s)
    links.drain()
    for wait in last:
        wait()


def sum_row(here, links, part, a_in, a_sum, a_side, b_in, b_sum, b_side, between):
    rows = part.shape[2]
    far = here.rings // 2
    n_b = rows - SUM_PART
    part_a, part_b = pl.ds(0, SUM_PART), pl.ds(SUM_PART, n_b)
    waits = {}

    def half(count, cut, sign):
        return pl.ds(0, cut) if sign > 0 else pl.ds(cut, count - cut)

    def mine(y_off, z_off, where):
        index = here.row_at(y_off, z_off)
        return part[lax.div(index, 2), lax.rem(index, 2), where]

    def ring_send(key, hop, total, partial_in, sums):
        cut = SUM_CUTS[0] if key[0] == "A" else SUM_CUTS[1]
        count = partial_in.shape[2]
        for n, s in enumerate((1, -1)):
            at, slot = sums.at[n, hop - 1], partial_in.at[n, hop - 1]
            if hop == far:
                sums[n, hop - 1] = total(s)
                where = half(count, cut, s)
                at, slot = at.at[where], slot.at[where]
            elif hop + 1 == far:
                sums[n, hop - 1] = total(s)
                where = half(count, cut, s)
                waits[key, s]()
                sums[n, hop - 1, where] = sums[n, hop - 1, where] + partial_in[n, hop, where]
            else:
                own = total(s)
                waits[key, s]()
                sums[n, hop - 1] = own + partial_in[n, hop]
            waits[key, s] = links.push(at, slot, here.ys[s], slot)

    def ring_end(key, own, partial_in):
        for s in (1, -1):
            waits[key, s]()
        return own.astype(F32) + partial_in[0, 0].astype(F32) + partial_in[1, 0].astype(F32)

    def a_send(j, hop):
        ring_send(("A", j), hop, lambda s: mine(s * hop, j, part_a), a_in.at[j], a_sum.at[j])

    side_waits = []

    def a_across(j):
        a_side[0, j - 1] = ring_end(("A", j), mine(0, j, part_a), a_in.at[j]).astype(BF16)
        slot = a_side.at[1, j - 1]
        side_waits.append(links.push(a_side.at[0, j - 1], slot, here.zls[j], slot))

    offsets = [far] + [s * h for h in range(far - 1, 0, -1) for s in (1, -1)] + [0]
    b_waits = {}

    def b_across():
        for i, y_off in enumerate(offsets):
            b_waits[y_off] = []
            for j in range(1, Z_LO):
                slot = b_side.at[i, j - 1]
                source = chunk(part, here.row_at(y_off, j), part_b)
                b_waits[y_off].append(links.push(source, slot, here.zls[j], slot))

    def b_total(y_off):
        i = offsets.index(y_off)
        for wait in b_waits[y_off]:
            wait()
        b_waits[y_off] = []
        return mine(y_off, 0, part_b).astype(F32) + b_side[i, 0].astype(F32) + b_side[i, 1].astype(F32)

    def b_send(hop):
        ring_send(
            ("B", 0), hop, lambda s: b_total(far if hop == far else s * hop).astype(BF16), b_in, b_sum
        )

    a_send(1, far)
    a_send(2, far)
    b_across()
    a_send(0, far)
    between()
    for hop in range(far - 1, 0, -1):
        a_send(1, hop)
        a_send(2, hop)
        if hop + 2 <= far:
            b_send(hop + 2)
        if hop + 1 < far:
            a_send(0, hop + 1)
        between()
    a_across(1)
    a_across(2)
    b_send(2)
    a_send(0, 1)
    between()
    b_send(1)
    total_a = ring_end(("A", 0), mine(0, 0, part_a), a_in.at[0])
    total_b = ring_end(("B", 0), b_total(0), b_in)
    for j, wait in enumerate(side_waits):
        wait()
        total_a += a_side[1, j].astype(F32)
    return total_a.astype(BF16), total_b.astype(BF16)


def weight_sum(here, links, scale, w_half, w_out, w_core, w_y_out, w_y, w_x_out, w_x, w_lo, w_hi, w_all):
    core, y, x = here.core, here.y, here.x
    fine = w_x.shape[1]

    def pair():
        w_out[...] = w_half[1 - core].astype(BF16)
        return [links.push(w_out, w_core, here.sibling, w_core)]

    def over_y():
        w_half[core] = w_half[core] + w_core[...].astype(F32)
        w_y_out[...] = w_half[core].astype(BF16)
        return [
            links.push(w_y_out.at[wrap(y + j, here.rings)], w_y.at[j - 1], here.ys[j], w_y.at[j - 1])
            for j in range(1, here.rings)
        ]

    def over_x():
        total = w_half[core, y]
        for j in range(1, here.rings):
            total += w_y[j - 1].astype(F32)
        w_half[core, y] = total
        for i in range(here.n_x):
            w_x_out[i] = total[i * fine : (i + 1) * fine].astype(BF16)
        return [
            links.push(w_x_out.at[wrap(x + j, here.n_x)], w_x.at[j - 1], here.xs[j], w_x.at[j - 1])
            for j in range(1, here.n_x)
        ]

    def over_lo():
        total = w_half[core, y, pl.ds(x * fine, fine)]
        for j in range(1, here.n_x):
            total += w_x[j - 1].astype(F32)
        w_lo[here.zl] = total
        slot = w_lo.at[here.zl]
        return [links.push(slot, slot, here.zls[j], w_lo.at[wrap(here.zl - j, Z_LO)]) for j in range(1, Z_LO)]

    def over_hi():
        w_hi[here.zh] = w_lo[0] + w_lo[1] + w_lo[2]
        slot = w_hi.at[here.zh]
        return [links.push(slot, slot, here.zhs[j], w_hi.at[wrap(here.zh - j, Z_HI)]) for j in range(1, Z_HI)]

    def back_y():
        total = (w_hi[0] + w_hi[1]) + (w_hi[2] + w_hi[3])
        w_all[core, x, y] = (total * scale).astype(BF16)
        slot = w_all.at[core, x, y]
        return [
            links.push(slot, slot, here.ys[j], w_all.at[core, x, wrap(y - j, here.rings)])
            for j in range(1, here.rings)
        ]

    def back_x():
        slot = w_all.at[core, x]
        return [
            links.push(slot, slot, here.xs[j], w_all.at[core, wrap(x - j, here.n_x)])
            for j in range(1, here.n_x)
        ]

    def back_pair():
        return [links.push(w_all.at[core], w_all.at[core], here.sibling, w_all.at[1 - core])]

    return [pair, over_y, over_x, over_lo, over_hi, back_y, back_x, back_pair]


def kernel(
    rings,
    n_x,
    scale,
    live,
    tile_rows,
    tile_cols,
    feat_ref,
    tiles_ref,
    weight_ref,
    cot_ref,
    hidden_ref,
    grad_feat_ref,
    grad_weight_ref,
    tiles,
    feats,
    total,
    part,
    from_core,
    sums,
    x_far,
    x_near,
    z_sums,
    z_far,
    z_near,
    grads,
    back,
    a_in,
    a_sum,
    a_side,
    b_in,
    b_sum,
    b_side,
    w_half,
    w_out,
    w_core,
    w_y_out,
    w_y,
    w_x_out,
    w_x,
    w_lo,
    w_hi,
    w_all,
    send,
    recv,
    local,
):
    here = Place(rings, n_x)
    links = Links(send, recv)
    load = pltpu.make_async_copy(tiles_ref, tiles, local)
    load.start()
    feats[lax.div(here.row, 2), lax.rem(here.row, 2)] = feat_ref[...]
    here.greet()
    gather_row(here, links, feats)
    load.wait()
    tile_products(tiles, feats, tile_rows, tile_cols, total, False)
    own_sum = sum_col(
        here,
        links,
        lambda target: target_sum(total, tile_rows, live, target),
        part,
        from_core,
        sums,
        x_far,
        x_near,
        z_sums,
        z_far,
        z_near,
    )
    pre_act = jnp.dot(own_sum, weight_ref[...], preferred_element_type=F32)
    gate = jax.nn.sigmoid(pre_act)
    own_grad = (cot_ref[...].astype(F32) * gate * (1.0 + pre_act * (1.0 - gate))).astype(BF16)
    grads[here.chip, here.core] = own_grad

    stages = weight_sum(
        here, links, scale, w_half, w_out, w_core, w_y_out, w_y, w_x_out, w_x, w_lo, w_hi, w_all
    )
    weight_waits = []

    def weight_step():
        for wait in weight_waits:
            wait()
        del weight_waits[:]
        if stages:
            weight_waits.extend(stages.pop(0)())

    def beside_gather():
        if len(stages) == 8:
            hidden_ref[...] = (pre_act * gate).astype(hidden_ref.dtype)
            term = lax.dot_general(own_sum, own_grad, (((0,), (0,)), ((), ())), preferred_element_type=F32)
            columns = term.shape[1] // 2
            for k in range(2):
                w_half[k] = term[:, k * columns : (k + 1) * columns].reshape(w_half.shape[1:])
        weight_step()

    gather_col(here, links, grads, beside_gather)
    tile_products(tiles, grads, tile_cols, tile_rows, total, True)
    rows, width = back.shape[2:]

    def store(target, _):
        back[target] = target_sum(total, tile_cols, live, target).astype(BF16).reshape(2, rows, width)
        return 0

    lax.fori_loop(0, back.shape[0], store, 0)
    parts = sum_row(here, links, back, a_in, a_sum, a_side, b_in, b_sum, b_side, weight_step)
    low = 0
    for chunk_sum in parts:
        count = chunk_sum.shape[0]
        grad_feat_ref[pl.ds(low, count)] = lax.dot_general(
            chunk_sum, weight_ref[...], (((1,), (1,)), ((), ())), preferred_element_type=F32
        ).astype(grad_feat_ref.dtype)
        low += count
    while stages or weight_waits:
        weight_step()
    columns = w_all.shape[-1]
    for k in range(2):
        for i in range(n_x):
            grad_weight_ref[:, i, :, k * columns : (k + 1) * columns] = w_all[k, i].astype(F32)
    links.drain()


def shards(features, tile_values, tile_rows, tile_cols, tile_live, weight, cotangent):
    rows, width = features.shape
    slots, edge, _ = tile_values.shape
    n_row, n_col = lax.axis_size("row"), lax.axis_size("col")
    rings, n_x = n_row // Z_LO, n_col // (2 * Z_HI)
    far, n_b = rings // 2, rows - SUM_PART
    columns, coarse = width // 2, width // rings
    fine = coarse // n_x
    vmem = pl.BlockSpec(memory_space=pltpu.VMEM)
    smem = pl.BlockSpec(memory_space=pltpu.SMEM)
    scratch = [
        pltpu.VMEM(shape, dtype)
        for shape, dtype in (
            ((slots, edge, edge), BF16),
            ((n_row // 2, 2, rows, width), BF16),
            ((slots + 1, edge, width), F32),
            ((n_col // 2, 2, rows, width), BF16),
            ((4, 4, rows, width), BF16),
            ((4, 4, rows, width), BF16),
            ((4, 2, 2, rows // 4, width), BF16),
            ((4, 2, 2, rows // 2, width), BF16),
            ((4, rows, width), BF16),
            ((2, rows // 2, width), BF16),
            ((2, rows, width), BF16),
            ((n_col // 2, 2, rows, width), BF16),
            ((n_row // 2, 2, rows, width), BF16),
            ((Z_LO, 2, far, SUM_PART, width), BF16),
            ((Z_LO, 2, far, SUM_PART, width), BF16),
            ((2, Z_LO - 1, SUM_PART, width), BF16),
            ((2, far, n_b, width), BF16),
            ((2, far, n_b, width), BF16),
            ((rings, Z_LO - 1, n_b, width), BF16),
            ((2, rings, coarse, columns), F32),
            ((rings, coarse, columns), BF16),
            ((rings, coarse, columns), BF16),
            ((rings, coarse, columns), BF16),
            ((rings - 1, coarse, columns), BF16),
            ((n_x, fine, columns), BF16),
            ((n_x - 1, fine, columns), BF16),
            ((Z_LO, fine, columns), F32),
            ((Z_HI, fine, columns), F32),
            ((2, n_x, rings, fine, columns), BF16),
        )
    ]
    hidden, grad_features, grad_weight = pl.pallas_call(
        functools.partial(kernel, rings, n_x, float(rows * n_row * n_col) ** -0.5),
        out_shape=(
            jax.ShapeDtypeStruct((rows, width), BF16),
            jax.ShapeDtypeStruct((rows, width), BF16),
            jax.ShapeDtypeStruct((rings, n_x, fine, width), F32),
        ),
        in_specs=[smem, smem, smem, vmem, pl.BlockSpec(memory_space=pl.ANY), vmem, vmem],
        out_specs=(vmem, vmem, vmem),
        scratch_shapes=scratch
        + [
            pltpu.SemaphoreType.DMA((320,)),
            pltpu.SemaphoreType.DMA((320,)),
            pltpu.SemaphoreType.DMA,
        ],
        compiler_params=pltpu.CompilerParams(
            collective_id=0, has_side_effects=True, vmem_limit_bytes=VMEM_LIMIT
        ),
        name="graph_layer",
    )(tile_live, tile_rows, tile_cols, features, tile_values, weight, cotangent)
    return hidden, grad_features, grad_weight.reshape(width, width)


def solution(mesh):
    return jax.shard_map(
        shards,
        mesh=mesh,
        in_specs=(
            P(("col", "row"), None),
            P(("row", "col"), None, None),
            P(("row", "col")),
            P(("row", "col")),
            P(("row", "col")),
            P(),
            P(("row", "col"), None),
        ),
        out_specs=(P(("row", "col"), None), P(("col", "row"), None), P()),
        check_vma=False,
    )
```

time: 1140 us -> 170 us (0.15)
  the two profiles are of different devices: /device:TPU:198 before, /device:TPU:1 now
where the time goes in v2:
time: 170 us; the launch traced here: 167 us
  Pallas kernels  160 us (94%)
  local copies, waits for them, and re-layouts  5.4 us (3%)
    pallas_call x1, Pallas kernels, shards(): pl.pallas_call(functools.partial(kernel, rings, n_x, float(rows * n_row *...  160 us
    unnamed x3, local copies, waits for them, and re-layouts  5.4 us

profile of v2, /device:TPU:1, one launch (start us, length us, event | category | flops | bytes accessed | tf_op | source)
XLA Modules:
  0.0 167.1 jit_solution(179183366521442280)
XLA Ops:
  1.3 160.5 %graph_layer.1 = (bf16[128,512]{1,0:T(8,128)(2,1)}, bf16[128,512]{1,0:T(8,128)(2,1)}, f32[8,4,16,512]{3,2,1,0:T(8,128)}) custom-call(s32[1]{0:T(128)S(6)} %copy.13.live, s32[16]{0:T(128)} %tile_rows.1, s32[16]{0:T(128)} %tile_cols.1, bf16[128,512]{1,0:T(8,128)(2,1)} %feat_ref.1, bf16[16,256,256]{2,1,0:T(8,128)(2,1)} %tiles_ref.1, ...), custom_call_target="tpu_custom_call" | custom-call | tf_op jit(solution)/shard_map/graph_layer/pallas_call | solution.py:672
  161.7 1.6 copy.14
  163.3 1.6 copy.15
  164.9 2.3 %copy.16 = f32[512,512]{1,0:T(8,128)} copy(f32[512,512]{1,0:T(8,128)} %bitcast.1) | data formatting | bytes 2097152

commit v3 on v2

--- a/solution.py
+++ b/solution.py
@@ -12,7 +12,7 @@
 BF16 = jnp.bfloat16
 Z_LO = 3
 Z_HI = 4
-VMEM_LIMIT = 58 * 1024 * 1024
+VMEM_LIMIT = 46 * 1024 * 1024
 GATHER_PART, GATHER_CUTS = 64, (32, 32)
 SUM_PART, SUM_CUTS = 80, (48, 16)
 
@@ -335,6 +335,7 @@
     between()
     for s in (1, -1):
         x_pass(2, s)
+    between()
     for s in (1, -1):
         x_end(2, s)
     links.drain()
@@ -518,6 +519,8 @@
     hidden_ref,
     grad_feat_ref,
     grad_weight_ref,
+    weight,
+    cot,
     tiles,
     feats,
     total,
@@ -553,12 +556,24 @@
 ):
     here = Place(rings, n_x)
     links = Links(send, recv)
-    load = pltpu.make_async_copy(tiles_ref, tiles, local)
-    load.start()
-    feats[lax.div(here.row, 2), lax.rem(here.row, 2)] = feat_ref[...]
+    loads = [
+        pltpu.make_async_copy(source, target, local.at[i])
+        for i, (source, target) in enumerate(
+            (
+                (feat_ref, chunk(feats, here.row)),
+                (tiles_ref, tiles),
+                (weight_ref, weight),
+                (cot_ref, cot),
+            )
+        )
+    ]
+    for load in loads:
+        load.start()
     here.greet()
+    loads[0].wait()
     gather_row(here, links, feats)
-    load.wait()
+    for load in loads[1:]:
+        load.wait()
     tile_products(tiles, feats, tile_rows, tile_cols, total, False)
     own_sum = sum_col(
         here,
@@ -573,9 +588,9 @@
         z_far,
         z_near,
     )
-    pre_act = jnp.dot(own_sum, weight_ref[...], preferred_element_type=F32)
+    pre_act = jnp.dot(own_sum, weight[...], preferred_element_type=F32)
     gate = jax.nn.sigmoid(pre_act)
-    own_grad = (cot_ref[...].astype(F32) * gate * (1.0 + pre_act * (1.0 - gate))).astype(BF16)
+    own_grad = (cot[...].astype(F32) * gate * (1.0 + pre_act * (1.0 - gate))).astype(BF16)
     grads[here.chip, here.core] = own_grad
 
     stages = weight_sum(
@@ -600,7 +615,9 @@
         weight_step()
 
     gather_col(here, links, grads, beside_gather)
+    weight_step()
     tile_products(tiles, grads, tile_cols, tile_rows, total, True)
+    weight_step()
     rows, width = back.shape[2:]
 
     def store(target, _):
@@ -613,7 +630,7 @@
     for chunk_sum in parts:
         count = chunk_sum.shape[0]
         grad_feat_ref[pl.ds(low, count)] = lax.dot_general(
-            chunk_sum, weight_ref[...], (((1,), (1,)), ((), ())), preferred_element_type=F32
+            chunk_sum, weight[...], (((1,), (1,)), ((), ())), preferred_element_type=F32
         ).astype(grad_feat_ref.dtype)
         low += count
     while stages or weight_waits:
@@ -638,6 +655,8 @@
     scratch = [
         pltpu.VMEM(shape, dtype)
         for shape, dtype in (
+            ((width, width), BF16),
+            ((rows, width), BF16),
             ((slots, edge, edge), BF16),
             ((n_row // 2, 2, rows, width), BF16),
             ((slots + 1, edge, width), F32),
@@ -676,13 +695,13 @@
             jax.ShapeDtypeStruct((rows, width), BF16),
             jax.ShapeDtypeStruct((rings, n_x, fine, width), F32),
         ),
-        in_specs=[smem, smem, smem, vmem, pl.BlockSpec(memory_space=pl.ANY), vmem, vmem],
+        in_specs=[smem] * 3 + [pl.BlockSpec(memory_space=pl.ANY)] * 4,
         out_specs=(vmem, vmem, vmem),
         scratch_shapes=scratch
         + [
             pltpu.SemaphoreType.DMA((320,)),
             pltpu.SemaphoreType.DMA((320,)),
-            pltpu.SemaphoreType.DMA,
+            pltpu.SemaphoreType.DMA((4,)),
         ],
         compiler_params=pltpu.CompilerParams(
             collective_id=0, has_side_effects=True, vmem_limit_bytes=VMEM_LIMIT

time: 170 us -> 160 us (0.941)
  Pallas kernels: 160 us -> 148 us
  local copies, waits for them, and re-layouts: 5.4 us -> 8.02 us
    pallas_call x1, Pallas kernels: 160 us -> 148 us  [shards(): pl.pallas_call(functools.partial(kernel, rings, n_x, float(rows * n_row *...]
    unnamed x3 -> x15, local copies, waits for them, and re-layouts: 5.4 us -> 8.02 us
where the time goes in v3:
time: 160 us; the launch traced here: 158 us
  Pallas kernels  148 us (92%)
  local copies, waits for them, and re-layouts  8.02 us (5%)
    pallas_call x1, Pallas kernels, shards(): pl.pallas_call(functools.partial(kernel, rings, n_x, float(rows * n_row *...  148 us
    unnamed x15, local copies, waits for them, and re-layouts  8.02 us

profile of v3, /device:TPU:1, one launch (start us, length us, event | category | flops | bytes accessed | tf_op | source)
XLA Modules:
  0.0 157.6 jit_solution(14588876378061001942)
XLA Ops:
  1.3 0.0 copy-start
  1.3 1.6 %copy-done = bf16[16,256,256]{2,1,0:T(8,128)(2,1)S(1)} copy-done((bf16[16,256,256]{2,1,0:T(8,128)(2,1)S(1)}, bf16[16,256,256]{2,1,0:T(8,128)(2,1)}, u32[]{:S(2)}) %copy-start) | copy-done | bytes 2097176
  2.9 0.0 copy-start.1
  2.9 1.0 copy-done.1
  3.9 0.0 copy-start.2
  3.9 0.9 copy-done.2
  4.8 0.0 copy-start.3
  4.8 0.9 copy-done.3
  5.7 0.0 copy-start.4
  5.7 0.7 copy-done.4
  6.4 0.0 copy-start.5
  6.4 0.7 copy-done.5
  7.0 148.3 %graph_layer.1 = (bf16[128,512]{1,0:T(8,128)(2,1)S(1)}, bf16[128,512]{1,0:T(8,128)(2,1)S(1)}, f32[8,4,16,512]{3,2,1,0:T(8,128)S(1)}) custom-call(s32[1]{0:T(128)S(6)} %copy.13.live, s32[16]{0:T(128)S(1)} %copy-done.4, s32[16]{0:T(128)S(1)} %copy-done.5, bf16[128,512]{1,0:T(8,128)(2,1)S(1)} %copy-done.2, bf16[16,256,256]{2,1,0:T(8,128)(2,1)S(1)} %copy-done, ...), custom_call_target="tpu_custom_call" | custom-call | tf_op jit(solution)/shard_map/graph_layer/pallas_call | solution.py:691
  155.3 0.7 copy.14
  156.0 0.7 copy.15
  156.6 1.0 copy.16
Async XLA Ops:
  1.3 1.6 %copy-start = (bf16[16,256,256]{2,1,0:T(8,128)(2,1)S(1)}, bf16[16,256,256]{2,1,0:T(8,128)(2,1)}, u32[]{:S(2)}) copy-start(bf16[16,256,256]{2,1,0:T(8,128)(2,1)} %tiles_ref.1) | copy-start | bytes 6291460
  2.9 1.0 copy-start.1
  3.9 0.9 copy-start.2
  4.8 0.9 copy-start.3
  5.7 0.7 copy-start.4
  6.4 0.7 copy-start.5

commit v4 on v3

--- a/solution.py
+++ b/solution.py
@@ -12,7 +12,7 @@
 BF16 = jnp.bfloat16
 Z_LO = 3
 Z_HI = 4
-VMEM_LIMIT = 46 * 1024 * 1024
+VMEM_LIMIT = 56 * 1024 * 1024
 GATHER_PART, GATHER_CUTS = 64, (32, 32)
 SUM_PART, SUM_CUTS = 80, (48, 16)
 
@@ -186,9 +186,10 @@
     halves = (pl.ds(0, half), pl.ds(half, half))
     core = here.core
     arrived = {}
-    for g, z_off in enumerate(ORDER):
+
+    def convert(g):
         for i, x_off in enumerate(ORDER):
-            chip = here.chip_at(x_off, z_off)
+            chip = here.chip_at(x_off, ORDER[g])
             part[chip] = tile(chip).astype(BF16).reshape(2, rows, width)
             slot = from_core.at[g, i]
             arrived[g, i] = links.push(part.at[chip, 1 - core], slot, here.sibling, slot)
@@ -240,10 +241,15 @@
             waits["z_near", s, h] = links.push(z_sums.at[g, halves[h]], slot, here.zhs[s], slot)
 
     blocks = [(0, 0), (0, 1), (1, 1), (2, 0), (1, 0), (2, 1), (3, 0), (3, 1)]
+    convert(0)
+    convert(1)
     x_first(blocks[0])
     x_first(blocks[1])
+    convert(2)
     for n, b in enumerate(blocks):
         x_second(b)
+        if n == 1:
+            convert(3)
         if n + 2 < len(blocks):
             x_first(blocks[n + 2])
         if n >= 1:
@@ -285,6 +291,8 @@
 
     def x_start(z_off, side):
         near[z_off, side] = {s: to_x(s, 0, z_off, piece[side]) for s in (1, -1)}
+        if z_off == 2:
+            near[z_off, side][2] = to_x(2, 0, z_off, piece[side])
 
     def x_pass(z_off, side):
         far[z_off, side] = {}
@@ -333,11 +341,14 @@
     for s in (1, -1):
         x_end(-s, -s)
     between()
-    for s in (1, -1):
-        x_pass(2, s)
+    for side in (1, -1):
+        for s in (1, -1):
+            near[2, side][s]()
+            to_core(-s, 2, piece[side])
     between()
-    for s in (1, -1):
-        x_end(2, s)
+    for side in (1, -1):
+        near[2, side][2]()
+        to_core(2, 2, piece[side])
     links.drain()
     for wait in last:
         wait()
@@ -419,7 +430,6 @@
     a_send(2, far)
     b_across()
     a_send(0, far)
-    between()
     for hop in range(far - 1, 0, -1):
         a_send(1, hop)
         a_send(2, hop)
@@ -516,9 +526,9 @@
     tiles_ref,
     weight_ref,
     cot_ref,
-    hidden_ref,
-    grad_feat_ref,
-    grad_weight_ref,
+    own_ref,
+    final_ref,
+    w_all,
     weight,
     cot,
     tiles,
@@ -549,7 +559,6 @@
     w_x,
     w_lo,
     w_hi,
-    w_all,
     send,
     recv,
     local,
@@ -607,7 +616,7 @@
 
     def beside_gather():
         if len(stages) == 8:
-            hidden_ref[...] = (pre_act * gate).astype(hidden_ref.dtype)
+            own_ref[...] = own_sum
             term = lax.dot_general(own_sum, own_grad, (((0,), (0,)), ((), ())), preferred_element_type=F32)
             columns = term.shape[1] // 2
             for k in range(2):
@@ -615,9 +624,7 @@
         weight_step()
 
     gather_col(here, links, grads, beside_gather)
-    weight_step()
     tile_products(tiles, grads, tile_cols, tile_rows, total, True)
-    weight_step()
     rows, width = back.shape[2:]
 
     def store(target, _):
@@ -625,21 +632,28 @@
         return 0
 
     lax.fori_loop(0, back.shape[0], store, 0)
+    weight_step()
     parts = sum_row(here, links, back, a_in, a_sum, a_side, b_in, b_sum, b_side, weight_step)
     low = 0
     for chunk_sum in parts:
         count = chunk_sum.shape[0]
-        grad_feat_ref[pl.ds(low, count)] = lax.dot_general(
-            chunk_sum, weight[...], (((1,), (1,)), ((), ())), preferred_element_type=F32
-        ).astype(grad_feat_ref.dtype)
+        final_ref[pl.ds(low, count)] = chunk_sum
         low += count
     while stages or weight_waits:
         weight_step()
-    columns = w_all.shape[-1]
+    links.drain()
+
+
+def results_kernel(own_ref, final_ref, sum_ref, weight_ref, hidden_ref, grad_feat_ref, grad_weight_ref):
+    pre_act = jnp.dot(own_ref[...], weight_ref[...], preferred_element_type=F32)
+    hidden_ref[...] = (pre_act * jax.nn.sigmoid(pre_act)).astype(hidden_ref.dtype)
+    grad_feat_ref[...] = lax.dot_general(
+        final_ref[...], weight_ref[...], (((1,), (1,)), ((), ())), preferred_element_type=F32
+    ).astype(grad_feat_ref.dtype)
+    columns = sum_ref.shape[-1]
     for k in range(2):
-        for i in range(n_x):
-            grad_weight_ref[:, i, :, k * columns : (k + 1) * columns] = w_all[k, i].astype(F32)
-    links.drain()
+        for i in range(sum_ref.shape[1]):
+            grad_weight_ref[:, i, :, k * columns : (k + 1) * columns] = sum_ref[k, i].astype(F32)
 
 
 def shards(features, tile_values, tile_rows, tile_cols, tile_live, weight, cotangent):
@@ -685,17 +699,16 @@
             ((n_x - 1, fine, columns), BF16),
             ((Z_LO, fine, columns), F32),
             ((Z_HI, fine, columns), F32),
-            ((2, n_x, rings, fine, columns), BF16),
         )
     ]
-    hidden, grad_features, grad_weight = pl.pallas_call(
+    own_sum, gathered_back, weight_total = pl.pallas_call(
         functools.partial(kernel, rings, n_x, float(rows * n_row * n_col) ** -0.5),
         out_shape=(
             jax.ShapeDtypeStruct((rows, width), BF16),
             jax.ShapeDtypeStruct((rows, width), BF16),
-            jax.ShapeDtypeStruct((rings, n_x, fine, width), F32),
+            jax.ShapeDtypeStruct((2, n_x, rings, fine, columns), BF16),
         ),
-        in_specs=[smem] * 3 + [pl.BlockSpec(memory_space=pl.ANY)] * 4,
+        in_specs=[smem] * 3 + [pl.BlockSpec(memory_space=pltpu.HBM)] * 4,
         out_specs=(vmem, vmem, vmem),
         scratch_shapes=scratch
         + [
@@ -708,6 +721,18 @@
         ),
         name="graph_layer",
     )(tile_live, tile_rows, tile_cols, features, tile_values, weight, cotangent)
+    hidden, grad_features, grad_weight = pl.pallas_call(
+        results_kernel,
+        out_shape=(
+            jax.ShapeDtypeStruct((rows, width), BF16),
+            jax.ShapeDtypeStruct((rows, width), BF16),
+            jax.ShapeDtypeStruct((rings, n_x, fine, width), F32),
+        ),
+        in_specs=[vmem] * 4,
+        out_specs=(vmem, vmem, vmem),
+        compiler_params=pltpu.CompilerParams(vmem_limit_bytes=VMEM_LIMIT),
+        name="results",
+    )(own_sum, gathered_back, weight_total, weight)
     return hidden, grad_features, grad_weight.reshape(width, width)
 
 

time: 160 us -> 154 us (0.963)
  local copies, waits for them, and re-layouts: 8.02 us -> 0 us
  Pallas kernels: 148 us -> 150 us
    unnamed x15 -> x0, local copies, waits for them, and re-layouts: 8.02 us -> none
    pallas_call x0 -> x1, Pallas kernels: none -> 2.76 us  [shards(): pl.pallas_call(results_kernel, out_shape=(jax.ShapeDtypeStruct((rows, wid...]
where the time goes in v4:
time: 154 us; the launch traced here: 151 us
  Pallas kernels  150 us (97%)
    pallas_call x1, Pallas kernels, shards(): pl.pallas_call(functools.partial(kernel, rings, n_x, float(rows * n_row *...  147 us

profile of v4, /device:TPU:1, one launch (start us, length us, event | category | flops | bytes accessed | tf_op | source)
XLA Modules:
  0.0 151.4 jit_solution(16505965596705556301)
XLA Ops:
  1.3 147.3 %graph_layer.1 = (bf16[128,512]{1,0:T(8,128)(2,1)}, bf16[128,512]{1,0:T(8,128)(2,1)}, bf16[2,4,8,16,256]{4,3,2,1,0:T(8,128)(2,1)}) custom-call(s32[1]{0:T(128)S(6)} %copy.10.live, s32[16]{0:T(128)} %tile_rows.1, s32[16]{0:T(128)} %tile_cols.1, bf16[128,512]{1,0:T(8,128)(2,1)} %feat_ref.1, bf16[16,256,256]{2,1,0:T(8,128)(2,1)} %tiles_ref.1, ...), custom_call_target="tpu_custom_call" | custom-call | tf_op jit(solution)/shard_map/graph_layer/pallas_call | solution.py:704
  148.6 2.8 %results.1 = (bf16[128,512]{1,0:T(8,128)(2,1)}, bf16[128,512]{1,0:T(8,128)(2,1)}, f32[8,4,16,512]{3,2,1,0:T(8,128)}) custom-call(bf16[128,512]{1,0:T(8,128)(2,1)} %get-tuple-element.9.own_ref, bf16[128,512]{1,0:T(8,128)(2,1)} %get-tuple-element.10.final_ref, bf16[2,4,8,16,256]{4,3,2,1,0:T(8,128)(2,1)} %get-tuple-element.11.sum_ref, bf16[512,512]{1,0:T(8,128)(2,1)} %weight_ref.3), custom_call_target="tpu_custom_call" | custom-call | tf_op jit(solution)/shard_map/results/pallas_call | solution.py:724

commit v5 on v4

--- a/solution.py
+++ b/solution.py
@@ -165,7 +165,7 @@
         )
         return 0
 
-    lax.fori_loop(0, slots, slot, 0)
+    lax.fori_loop(0, slots, slot, 0, unroll=True)
 
 
 def target_sum(total, into, live, target):
@@ -242,9 +242,9 @@
 
     blocks = [(0, 0), (0, 1), (1, 1), (2, 0), (1, 0), (2, 1), (3, 0), (3, 1)]
     convert(0)
-    convert(1)
     x_first(blocks[0])
     x_first(blocks[1])
+    convert(1)
     convert(2)
     for n, b in enumerate(blocks):
         x_second(b)
@@ -519,16 +519,19 @@
     rings,
     n_x,
     scale,
-    live,
-    tile_rows,
-    tile_cols,
+    live_ref,
+    rows_ref,
+    cols_ref,
     feat_ref,
     tiles_ref,
     weight_ref,
     cot_ref,
-    own_ref,
-    final_ref,
-    w_all,
+    own_out,
+    final_out,
+    weight_out,
+    live,
+    tile_rows,
+    tile_cols,
     weight,
     cot,
     tiles,
@@ -559,6 +562,9 @@
     w_x,
     w_lo,
     w_hi,
+    w_all,
+    own_ref,
+    final_ref,
     send,
     recv,
     local,
@@ -573,6 +579,9 @@
                 (tiles_ref, tiles),
                 (weight_ref, weight),
                 (cot_ref, cot),
+                (live_ref, live),
+                (rows_ref, tile_rows),
+                (cols_ref, tile_cols),
             )
         )
     ]
@@ -607,16 +616,26 @@
     )
     weight_waits = []
 
+    leaving = []
+
+    def leave(source, target):
+        copy = pltpu.make_async_copy(source, target, local.at[7 + len(leaving)])
+        copy.start()
+        leaving.append(copy)
+
     def weight_step():
         for wait in weight_waits:
             wait()
         del weight_waits[:]
         if stages:
             weight_waits.extend(stages.pop(0)())
+        elif len(leaving) == 1:
+            leave(w_all, weight_out)
 
     def beside_gather():
         if len(stages) == 8:
             own_ref[...] = own_sum
+            leave(own_ref, own_out)
             term = lax.dot_general(own_sum, own_grad, (((0,), (0,)), ((), ())), preferred_element_type=F32)
             columns = term.shape[1] // 2
             for k in range(2):
@@ -639,9 +658,10 @@
         count = chunk_sum.shape[0]
         final_ref[pl.ds(low, count)] = chunk_sum
         low += count
-    while stages or weight_waits:
-        weight_step()
+    leave(final_ref, final_out)
     links.drain()
+    for copy in leaving:
+        copy.wait()
 
 
 def results_kernel(own_ref, final_ref, sum_ref, weight_ref, hidden_ref, grad_feat_ref, grad_weight_ref):
@@ -666,6 +686,7 @@
     fine = coarse // n_x
     vmem = pl.BlockSpec(memory_space=pltpu.VMEM)
     smem = pl.BlockSpec(memory_space=pltpu.SMEM)
+    hbm = pl.BlockSpec(memory_space=pltpu.HBM)
     scratch = [
         pltpu.VMEM(shape, dtype)
         for shape, dtype in (
@@ -699,6 +720,9 @@
             ((n_x - 1, fine, columns), BF16),
             ((Z_LO, fine, columns), F32),
             ((Z_HI, fine, columns), F32),
+            ((2, n_x, rings, fine, columns), BF16),
+            ((rows, width), BF16),
+            ((rows, width), BF16),
         )
     ]
     own_sum, gathered_back, weight_total = pl.pallas_call(
@@ -708,13 +732,14 @@
             jax.ShapeDtypeStruct((rows, width), BF16),
             jax.ShapeDtypeStruct((2, n_x, rings, fine, columns), BF16),
         ),
-        in_specs=[smem] * 3 + [pl.BlockSpec(memory_space=pltpu.HBM)] * 4,
-        out_specs=(vmem, vmem, vmem),
-        scratch_shapes=scratch
+        in_specs=[hbm] * 7,
+        out_specs=(hbm, hbm, hbm),
+        scratch_shapes=[pltpu.SMEM((n,), jnp.int32) for n in (1, slots, slots)]
+        + scratch
         + [
             pltpu.SemaphoreType.DMA((320,)),
             pltpu.SemaphoreType.DMA((320,)),
-            pltpu.SemaphoreType.DMA((4,)),
+            pltpu.SemaphoreType.DMA((10,)),
         ],
         compiler_params=pltpu.CompilerParams(
             collective_id=0, has_side_effects=True, vmem_limit_bytes=VMEM_LIMIT

time: 154 us -> 147 us (0.955)
  Pallas kernels: 150 us -> 144 us
    pallas_call x1, Pallas kernels: 147 us -> 141 us  [shards(): pl.pallas_call(functools.partial(kernel, rings, n_x, float(rows * n_row *...]
where the time goes in v5:
time: 147 us; the launch traced here: 145 us
  Pallas kernels  144 us (98%)
    pallas_call x1, Pallas kernels, shards(): pl.pallas_call(functools.partial(kernel, rings, n_x, float(rows * n_row *...  141 us

profile of v5, /device:TPU:1, one launch (start us, length us, event | category | flops | bytes accessed | tf_op | source)
XLA Modules:
  0.0 145.2 jit_solution(11560025327698993478)
XLA Ops:
  1.3 141.2 %graph_layer.1 = (bf16[128,512]{1,0:T(8,128)(2,1)}, bf16[128,512]{1,0:T(8,128)(2,1)}, bf16[2,4,8,16,256]{4,3,2,1,0:T(8,128)(2,1)}) custom-call(s32[1]{0:T(128)S(6)} %copy.10.live_ref, s32[16]{0:T(128)} %rows_ref.1, s32[16]{0:T(128)} %cols_ref.1, bf16[128,512]{1,0:T(8,128)(2,1)} %feat_ref.1, bf16[16,256,256]{2,1,0:T(8,128)(2,1)} %tiles_ref.1, ...), custom_call_target="tpu_custom_call" | custom-call | tf_op jit(solution)/shard_map/graph_layer/pallas_call | solution.py:728
  142.5 2.8 %results.1 = (bf16[128,512]{1,0:T(8,128)(2,1)}, bf16[128,512]{1,0:T(8,128)(2,1)}, f32[8,4,16,512]{3,2,1,0:T(8,128)}) custom-call(bf16[128,512]{1,0:T(8,128)(2,1)} %get-tuple-element.9.own_ref, bf16[128,512]{1,0:T(8,128)(2,1)} %get-tuple-element.10.final_ref, bf16[2,4,8,16,256]{4,3,2,1,0:T(8,128)(2,1)} %get-tuple-element.11.sum_ref, bf16[512,512]{1,0:T(8,128)(2,1)} %weight_ref.3), custom_call_target="tpu_custom_call" | custom-call | tf_op jit(solution)/shard_map/results/pallas_call | solution.py:749
